TPU v7x, 512 devices: a whole 4x4x16 slice. The times are simulated.
512 devices in a mesh: gx: 32 (over z, core), gy: 16 (over y, x).
Axes of the slice: x: 4, y: 4, z: 16, core: 2. Of those that a mesh axis runs over, the one named last changes fastest.
Arguments:
- source: float32 [256, 2048, 256], P('gx', 'gy'), may hold values from -8 to 8
- density: float32 [256, 2048, 256], P('gx', 'gy'), may hold values from 0.08 to 1.7
Outputs:
- pressure: float32 [256, 2048, 256], P('gx', 'gy')
- residual: float32 [256, 2048, 256], P('gx', 'gy')
All inputs are finite; a program needn't handle non-finite values.
Results may differ from a plain program's by a relative error of at most 0.00021.
Values sent between devices are 32-bit elements; how exact they have to be, the bound alone decides.
A program may use at most 64 MiB of HBM per device.

v0:
```python
import jax
import jax.numpy as jnp
from jax import lax
from jax.sharding import PartitionSpec as P

ITERS = 2


def extended(shard, sides, width):
    for axis, dim in sides:
        devices, length = (lax.axis_size(axis), shard.shape[dim])
        up = [(i, (i + 1) % devices) for i in range(devices - 1)]
        down = [(j, i) for i, j in up]
        last = lax.slice_in_dim(shard, length - width, length, axis=dim)
        initial = lax.slice_in_dim(shard, 0, width, axis=dim)
        before = lax.ppermute(last, axis, up)
        after = lax.ppermute(initial, axis, down)
        shard = jnp.concatenate([before, shard, after], axis=dim)
    return shard


def neighbours(padded):
    return [
        padded[2:, 1:-1, 1:-1],
        padded[:-2, 1:-1, 1:-1],
        padded[1:-1, 2:, 1:-1],
        padded[1:-1, :-2, 1:-1],
        padded[1:-1, 1:-1, 2:],
        padded[1:-1, 1:-1, :-2],
    ]


def pad_depth(field):
    return jnp.pad(field, ((0, 0), (0, 0), (1, 1)))


def weights_from(center, padded):
    nearby = neighbours(pad_depth(padded))
    weights = [2.0 / jnp.where(center > 0, center + other, 1.0) for other in nearby]
    diag_sum = weights[0]
    for weight_one in weights[1:]:
        diag_sum = diag_sum + weight_one
    return (weights, lax.rsqrt(diag_sum))


def couple(padded, weights):
    nearby = neighbours(pad_depth(padded))
    total = weights[0] * nearby[0]
    for weight_one, other in zip(weights[1:], nearby[1:]):
        total = total + weight_one * other
    return total


def scaled_apply(field, weights, scale_inv):
    scaled = scale_inv * field
    padded = extended(scaled, (("gx", 0), ("gy", 1)), 1)
    return field - scale_inv * couple(padded, weights)


def inner_pair(residual, shadow):
    gamma_part = jnp.sum(residual * residual)
    delta_part = jnp.sum(shadow * residual)
    return lax.psum((gamma_part, delta_part), ("gx", "gy"))


def shards(source, density):
    rim_density = extended(density, (("gx", 0), ("gy", 1)), 1)
    weights, scale_inv = weights_from(density, rim_density)
    residual = scale_inv * source
    shadow = scaled_apply(residual, weights, scale_inv)
    solution = jnp.zeros_like(source)
    direction = jnp.zeros_like(source)
    along = jnp.zeros_like(source)
    pushed = jnp.zeros_like(source)
    gamma_old = jnp.float32(1.0)
    alpha_old = jnp.float32(1.0)
    for iteration in range(ITERS):
        gamma_now, delta_now = inner_pair(residual, shadow)
        fresh = scaled_apply(shadow, weights, scale_inv)
        if iteration == 0:
            beta_now = jnp.float32(0.0)
            alpha_now = gamma_now / delta_now
        else:
            beta_now = gamma_now / gamma_old
            alpha_now = gamma_now / (delta_now - beta_now * gamma_now / alpha_old)
        pushed = fresh + beta_now * pushed
        along = shadow + beta_now * along
        direction = residual + beta_now * direction
        solution = solution + alpha_now * direction
        residual = residual - alpha_now * along
        shadow = shadow - alpha_now * pushed
        gamma_old = gamma_now
        alpha_old = alpha_now
    return (scale_inv * solution, residual)


def solution(mesh):
    in_specs = (P("gx", "gy", None), P("gx", "gy", None))
    out_specs = (P("gx", "gy", None), P("gx", "gy", None))
    return jax.shard_map(shards, mesh=mesh, in_specs=in_specs, out_specs=out_specs, check_vma=False)
```

profile of v0, /device:TPU:1, one launch (start us, length us, event | category | flops | bytes accessed | tf_op | source)
XLA Modules:
  0.0 292.1 jit_solution(12491736023000275440)
XLA Ops:
  1.6 4.9 %collective-permute-start.1 = (f32[1,128,256]{2,1,0:T(8,128)S(1)}, f32[1,128,256]{2,1,0:T(8,128)S(1)}, u32[]{:S(2)}, u32[]{:S(2)}) collective-permute-start(f32[1,128,256]{2,1,0:T(8,128)S(1)} %get-tuple-element.30), channel_id=1, source_target_pairs={{0,16},{16,32},{32,48},{48,64},{64,80},{80,96},{96,112},{112,128},... | collective-permute-start | bytes 393224 | tf_op jit(solution)/shard_map/ppermute | solution.py:16
  6.6 5.1 %collective-permute-start = (f32[1,128,256]{2,1,0:T(8,128)S(1)}, f32[1,128,256]{2,1,0:T(8,128)S(1)}, u32[]{:S(2)}, u32[]{:S(2)}) collective-permute-start(f32[1,128,256]{2,1,0:T(8,128)S(1)} %get-tuple-element.29), channel_id=1, source_target_pairs={{16,0},{32,16},{48,32},{64,48},{80,64},{96,80},{112,96},{128,112},... | collective-permute-start | bytes 393224 | tf_op jit(solution)/shard_map/ppermute | solution.py:17
  11.7 1.3 constant_dynamic-update-slice_fusion.1
  13.1 2.9 collective-permute-start.3
  16.0 1.3 collective-permute-start.2
  17.3 3.1 %collective-permute-done.2 = f32[10,1,256]{2,1,0:T(1,128)S(1)} collective-permute-done((f32[10,1,256]{2,1,0:T(1,128)S(1)}, f32[10,1,256]{2,1,0:T(1,128)S(1)}, u32[]{:S(2)}, u32[]{:S(2)}) %collective-permute-start.2) | collective-permute-done | bytes 10272 | tf_op jit(solution)/shard_map/ppermute | solution.py:17
  21.2 2.2 fusion.43
  23.5 3.3 %collective-permute-start.5 = (f32[1,128,256]{2,1,0:T(8,128)S(1)}, f32[1,128,256]{2,1,0:T(8,128)S(1)}, u32[]{:S(2)}, u32[]{:S(2)}) collective-permute-start(f32[1,128,256]{2,1,0:T(8,128)S(1)} %get-tuple-element.27), channel_id=1, source_target_pairs={{0,16},{16,32},{32,48},{48,64},{64,80},{80,96},{96,112},{112,128},... | collective-permute-start | bytes 393224 | tf_op jit(solution)/shard_map/ppermute | solution.py:16
  26.8 1.9 collective-permute-start.4
  28.8 4.3 %collective-permute-done.4 = f32[1,128,256]{2,1,0:T(8,128)S(1)} collective-permute-done((f32[1,128,256]{2,1,0:T(8,128)S(1)}, f32[1,128,256]{2,1,0:T(8,128)S(1)}, u32[]{:S(2)}, u32[]{:S(2)}) %collective-permute-start.4) | collective-permute-done | bytes 131104 | tf_op jit(solution)/shard_map/ppermute | solution.py:17
  33.1 3.1 %collective-permute-start.7 = (f32[10,1,256]{2,1,0:T(1,128)S(1)}, f32[10,1,256]{2,1,0:T(1,128)S(1)}, u32[]{:S(2)}, u32[]{:S(2)}) collective-permute-start(f32[10,1,256]{2,1,0:T(1,128)S(1)} %get-tuple-element.21), channel_id=1, source_target_pairs={{0,1},{1,2},{2,3},{3,4},{4,5},{5,6},{6,7},{7,8},{8,9},{9,10},{10,1... | collective-permute-start | bytes 30728 | tf_op jit(solution)/shard_map/ppermute | solution.py:16
  36.3 1.3 collective-permute-start.6
  37.6 3.1 %collective-permute-done.6 = f32[10,1,256]{2,1,0:T(1,128)S(1)} collective-permute-done((f32[10,1,256]{2,1,0:T(1,128)S(1)}, f32[10,1,256]{2,1,0:T(1,128)S(1)}, u32[]{:S(2)}, u32[]{:S(2)}) %collective-permute-start.6) | collective-permute-done | bytes 10272 | tf_op jit(solution)/shard_map/ppermute | solution.py:17
  41.4 3.4 %multiply_reduce_fusion.2 = (f32[]{:T(128)}, f32[]{:T(128)}, f32[8,128,256]{2,1,0:T(8,128)S(1)}) fusion(f32[8,128,256]{2,1,0:T(8,128)S(1)} %get-tuple-element.13, f32[8,128,256]{2,1,0:T(8,128)S(1)} %get-tuple-element.14, f32[10,130,258]{2,1,0:T(8,128)S(1)} %select_maximum_fusion.4, f32[8,128,256]{2,1,0:T(8,128)S(1)} %copy-done, ...), kind=kLoop, calls=%fused_computation.84 | loop fusion | flops 10485758 | bytes 12079112 | tf_op jit(solution)/shard_map/reduce_sum | solution.py:62
  45.1 3.2 %collective-permute-start.9 = (f32[1,128,256]{2,1,0:T(8,128)S(1)}, f32[1,128,256]{2,1,0:T(8,128)S(1)}, u32[]{:S(2)}, u32[]{:S(2)}) collective-permute-start(f32[1,128,256]{2,1,0:T(8,128)S(1)} %get-tuple-element.25), channel_id=1, source_target_pairs={{0,16},{16,32},{32,48},{48,64},{64,80},{80,96},{96,112},{112,128},... | collective-permute-start | bytes 393224 | tf_op jit(solution)/shard_map/ppermute | solution.py:16
  48.3 1.9 collective-permute-start.8
  50.2 4.3 %collective-permute-done.8 = f32[1,128,256]{2,1,0:T(8,128)S(1)} collective-permute-done((f32[1,128,256]{2,1,0:T(8,128)S(1)}, f32[1,128,256]{2,1,0:T(8,128)S(1)}, u32[]{:S(2)}, u32[]{:S(2)}) %collective-permute-start.8) | collective-permute-done | bytes 131104 | tf_op jit(solution)/shard_map/ppermute | solution.py:17
  55.2 4.4 %collective-permute-start.11 = (f32[10,1,256]{2,1,0:T(1,128)}, f32[10,1,256]{2,1,0:T(1,128)S(1)}, u32[]{:S(2)}, u32[]{:S(2)}) collective-permute-start(f32[10,1,256]{2,1,0:T(1,128)} %get-tuple-element.19), channel_id=1, source_target_pairs={{0,1},{1,2},{2,3},{3,4},{4,5},{5,6},{6,7},{7,8},{8,9},{9,10},{10,1... | collective-permute-start | bytes 30728 | tf_op jit(solution)/shard_map/ppermute | solution.py:16
  59.6 1.3 collective-permute-start.10
  60.9 114.2 %all-reduce.4 = (f32[]{:T(128)}, f32[]{:T(128)}) all-reduce(f32[]{:T(128)} %get-tuple-element.5, f32[]{:T(128)} %get-tuple-element.4), channel_id=1, replica_groups=mesh['gx'=32,'gy'=16] {'gx','gy'}, use_global_device_ids=true, to_apply=%region_1.2 | all-reduce | flops 2 | bytes 16 | tf_op jit(solution)/shard_map/psum | solution.py:63
  176.5 2.2 select_maximum_fusion
  178.7 5.7 %multiply_reduce_fusion = (f32[]{:T(128)}, f32[]{:T(128)}, f32[8,128,256]{2,1,0:T(8,128)}) fusion(f32[8,128,256]{2,1,0:T(8,128)S(1)} %copy-done.5, f32[8,128,256]{2,1,0:T(8,128)} %copy-done.6, f32[]{:T(128)S(6)} %div.36, f32[8,128,256]{2,1,0:T(8,128)S(1)} %get-tuple-element.14, f32[10,130,258]{2,1,0:T(8,128)S(1)} %select_maximum_fusion, ...), kind=kLoop, calls=%fused_computation.81 | loop fusion | flops 11534334 | bytes 13127692 | tf_op jit(solution)/shard_map/reduce_sum | solution.py:62
  184.4 99.5 %all-reduce.3 = (f32[]{:T(128)}, f32[]{:T(128)}) all-reduce(f32[]{:T(128)} %get-tuple-element.3, f32[]{:T(128)} %get-tuple-element.2), channel_id=1, replica_groups=mesh['gx'=32,'gy'=16] {'gx','gy'}, use_global_device_ids=true, to_apply=%region_5.6 | all-reduce | flops 2 | bytes 16 | tf_op jit(solution)/shard_map/psum | solution.py:63
  288.5 3.6 %multiply_subtract_fusion = (f32[8,128,256]{2,1,0:T(8,128)}, f32[8,128,256]{2,1,0:T(8,128)}) fusion(f32[8,128,256]{2,1,0:T(8,128)} %get-tuple-element.10, f32[8,128,256]{2,1,0:T(8,128)} %copy-done.6, f32[]{:T(128)S(6)} %div.37, f32[]{:T(128)S(6)} %div.39, f32[8,128,256]{2,1,0:T(8,128)} %copy-done.4, f32[]{:T(128)S(6)} %div.36, ...), kind=kLoop, calls=%fused_computation.79 | loop fusion | flops 3145728 | bytes 6291468 | tf_op jit(solution)/shard_map/sub | solution.py:90
  (43 shorter events, 3.4 us)
Async XLA Ops:
  1.6 10.1 %collective-permute-start.1 = (f32[1,128,256]{2,1,0:T(8,128)S(1)}, f32[1,128,256]{2,1,0:T(8,128)S(1)}, u32[]{:S(2)}, u32[]{:S(2)}) collective-permute-start(f32[1,128,256]{2,1,0:T(8,128)S(1)} %get-tuple-element.30), channel_id=1, source_target_pairs={{0,16},{16,32},{32,48},{48,64},{64,80},{80,96},{96,112},{112,128},... | collective-permute-start | bytes 393224 | tf_op jit(solution)/shard_map/ppermute | solution.py:16
  6.6 6.5 %collective-permute-start = (f32[1,128,256]{2,1,0:T(8,128)S(1)}, f32[1,128,256]{2,1,0:T(8,128)S(1)}, u32[]{:S(2)}, u32[]{:S(2)}) collective-permute-start(f32[1,128,256]{2,1,0:T(8,128)S(1)} %get-tuple-element.29), channel_id=1, source_target_pairs={{16,0},{32,16},{48,32},{64,48},{80,64},{96,80},{112,96},{128,112},... | collective-permute-start | bytes 393224 | tf_op jit(solution)/shard_map/ppermute | solution.py:17
  13.1 8.1 %copy-start = (f32[8,128,256]{2,1,0:T(8,128)S(1)}, f32[8,128,256]{2,1,0:T(8,128)}, u32[]{:S(2)}) copy-start(f32[8,128,256]{2,1,0:T(8,128)} %param.3) | copy-start | bytes 3145732
  13.1 8.1 %copy-start.11 = (f32[8,128,256]{2,1,0:T(8,128)S(1)}, f32[8,128,256]{2,1,0:T(8,128)}, u32[]{:S(2)}) copy-start(f32[8,128,256]{2,1,0:T(8,128)} %param.2) | copy-start | bytes 3145732
  13.1 4.2 %collective-permute-start.3 = (f32[10,1,256]{2,1,0:T(1,128)S(1)}, f32[10,1,256]{2,1,0:T(1,128)S(1)}, u32[]{:S(2)}, u32[]{:S(2)}) collective-permute-start(f32[10,1,256]{2,1,0:T(1,128)S(1)} %get-tuple-element.23), channel_id=1, source_target_pairs={{0,1},{1,2},{2,3},{3,4},{4,5},{5,6},{6,7},{7,8},{8,9},{9,10},{10,1... | collective-permute-start | bytes 30728 | tf_op jit(solution)/shard_map/ppermute | solution.py:16
  16.0 4.4 %collective-permute-start.2 = (f32[10,1,256]{2,1,0:T(1,128)S(1)}, f32[10,1,256]{2,1,0:T(1,128)S(1)}, u32[]{:S(2)}, u32[]{:S(2)}) collective-permute-start(f32[10,1,256]{2,1,0:T(1,128)S(1)} %get-tuple-element.24), channel_id=1, source_target_pairs={{1,0},{2,1},{3,2},{4,3},{5,4},{6,5},{7,6},{8,7},{9,8},{10,9},{11,1... | collective-permute-start | bytes 30728 | tf_op jit(solution)/shard_map/ppermute | solution.py:17
  23.4 18.0 %copy-start.4 = (f32[8,128,256]{2,1,0:T(8,128)}, f32[8,128,256]{2,1,0:T(8,128)S(1)}, u32[]{:S(2)}) copy-start(f32[8,128,256]{2,1,0:T(8,128)S(1)} %get-tuple-element.13) | copy-start | bytes 3145732
  23.4 18.0 %copy-start.7 = (f32[8,128,256]{2,1,0:T(8,128)}, f32[8,128,256]{2,1,0:T(8,128)S(1)}, u32[]{:S(2)}) copy-start(f32[8,128,256]{2,1,0:T(8,128)S(1)} %get-tuple-element.15) | copy-start | bytes 3145732
  23.4 18.0 %copy-start.8 = (f32[8,128,256]{2,1,0:T(8,128)}, f32[8,128,256]{2,1,0:T(8,128)S(1)}, u32[]{:S(2)}) copy-start(f32[8,128,256]{2,1,0:T(8,128)S(1)} %get-tuple-element.16) | copy-start | bytes 3145732
  23.5 5.3 %collective-permute-start.5 = (f32[1,128,256]{2,1,0:T(8,128)S(1)}, f32[1,128,256]{2,1,0:T(8,128)S(1)}, u32[]{:S(2)}, u32[]{:S(2)}) collective-permute-start(f32[1,128,256]{2,1,0:T(8,128)S(1)} %get-tuple-element.27), channel_id=1, source_target_pairs={{0,16},{16,32},{32,48},{48,64},{64,80},{80,96},{96,112},{112,128},... | collective-permute-start | bytes 393224 | tf_op jit(solution)/shard_map/ppermute | solution.py:16
  26.8 6.3 %collective-permute-start.4 = (f32[1,128,256]{2,1,0:T(8,128)S(1)}, f32[1,128,256]{2,1,0:T(8,128)S(1)}, u32[]{:S(2)}, u32[]{:S(2)}) collective-permute-start(f32[1,128,256]{2,1,0:T(8,128)S(1)} %get-tuple-element.28), channel_id=1, source_target_pairs={{16,0},{32,16},{48,32},{64,48},{80,64},{96,80},{112,96},{128,112},... | collective-permute-start | bytes 393224 | tf_op jit(solution)/shard_map/ppermute | solution.py:17
  33.1 4.4 %collective-permute-start.7 = (f32[10,1,256]{2,1,0:T(1,128)S(1)}, f32[10,1,256]{2,1,0:T(1,128)S(1)}, u32[]{:S(2)}, u32[]{:S(2)}) collective-permute-start(f32[10,1,256]{2,1,0:T(1,128)S(1)} %get-tuple-element.21), channel_id=1, source_target_pairs={{0,1},{1,2},{2,3},{3,4},{4,5},{5,6},{6,7},{7,8},{8,9},{9,10},{10,1... | collective-permute-start | bytes 30728 | tf_op jit(solution)/shard_map/ppermute | solution.py:16
  36.3 4.4 %collective-permute-start.6 = (f32[10,1,256]{2,1,0:T(1,128)S(1)}, f32[10,1,256]{2,1,0:T(1,128)S(1)}, u32[]{:S(2)}, u32[]{:S(2)}) collective-permute-start(f32[10,1,256]{2,1,0:T(1,128)S(1)} %get-tuple-element.22), channel_id=1, source_target_pairs={{1,0},{2,1},{3,2},{4,3},{5,4},{6,5},{7,6},{8,7},{9,8},{10,9},{11,1... | collective-permute-start | bytes 30728 | tf_op jit(solution)/shard_map/ppermute | solution.py:17
  44.9 10.4 %copy-start.6 = (f32[8,128,256]{2,1,0:T(8,128)}, f32[8,128,256]{2,1,0:T(8,128)S(1)}, u32[]{:S(2)}) copy-start(f32[8,128,256]{2,1,0:T(8,128)S(1)} %get-tuple-element.11) | copy-start | bytes 3145732
  45.0 9.5 %copy-start.2 = (f32[8,128,256]{2,1,0:T(8,128)}, f32[8,128,256]{2,1,0:T(8,128)S(1)}, u32[]{:S(2)}) copy-start(f32[8,128,256]{2,1,0:T(8,128)S(1)} %mul.118) | copy-start | bytes 3145732
  45.1 5.2 %collective-permute-start.9 = (f32[1,128,256]{2,1,0:T(8,128)S(1)}, f32[1,128,256]{2,1,0:T(8,128)S(1)}, u32[]{:S(2)}, u32[]{:S(2)}) collective-permute-start(f32[1,128,256]{2,1,0:T(8,128)S(1)} %get-tuple-element.25), channel_id=1, source_target_pairs={{0,16},{16,32},{32,48},{48,64},{64,80},{80,96},{96,112},{112,128},... | collective-permute-start | bytes 393224 | tf_op jit(solution)/shard_map/ppermute | solution.py:16
  48.3 6.3 %collective-permute-start.8 = (f32[1,128,256]{2,1,0:T(8,128)S(1)}, f32[1,128,256]{2,1,0:T(8,128)S(1)}, u32[]{:S(2)}, u32[]{:S(2)}) collective-permute-start(f32[1,128,256]{2,1,0:T(8,128)S(1)} %get-tuple-element.26), channel_id=1, source_target_pairs={{16,0},{32,16},{48,32},{64,48},{80,64},{96,80},{112,96},{128,112},... | collective-permute-start | bytes 393224 | tf_op jit(solution)/shard_map/ppermute | solution.py:17
  54.6 0.7 copy-start.9
  55.2 121.2 %collective-permute-start.11 = (f32[10,1,256]{2,1,0:T(1,128)}, f32[10,1,256]{2,1,0:T(1,128)S(1)}, u32[]{:S(2)}, u32[]{:S(2)}) collective-permute-start(f32[10,1,256]{2,1,0:T(1,128)} %get-tuple-element.19), channel_id=1, source_target_pairs={{0,1},{1,2},{2,3},{3,4},{4,5},{5,6},{6,7},{7,8},{8,9},{9,10},{10,1... | collective-permute-start | bytes 30728 | tf_op jit(solution)/shard_map/ppermute | solution.py:16
  59.6 116.8 %collective-permute-start.10 = (f32[10,1,256]{2,1,0:T(1,128)}, f32[10,1,256]{2,1,0:T(1,128)S(1)}, u32[]{:S(2)}, u32[]{:S(2)}) collective-permute-start(f32[10,1,256]{2,1,0:T(1,128)} %get-tuple-element.20), channel_id=1, source_target_pairs={{1,0},{2,1},{3,2},{4,3},{5,4},{6,5},{7,6},{8,7},{9,8},{10,9},{11,1... | collective-permute-start | bytes 30728 | tf_op jit(solution)/shard_map/ppermute | solution.py:17
  176.4 2.2 copy-start.1
  176.4 2.2 copy-start.3
  176.4 2.2 copy-start.5
  176.4 2.2 copy-start.10
where the time goes:
time: 293 us; the launch traced here: 292 us
  blocking collectives  214 us (73%)
  starting transfers between devices  34.8 us (12%)
  other arithmetic  19.4 us (7%)
  waiting for transfers between devices  14.9 us (5%)
  between operations  6.86 us (2%)
    psum x2, blocking collectives, inner_pair(): return lax.psum((gamma_part, delta_part), ('gx', 'gy'))  214 us
    ppermute x6, starting transfers between devices, extended(): before = lax.ppermute(last, axis, up)  21.9 us
    ppermute x6, waiting for transfers between devices, extended(): after = lax.ppermute(initial, axis, down)  14.9 us
    ppermute x6, starting transfers between devices, extended(): after = lax.ppermute(initial, axis, down)  12.9 us
    reduce_sum x2, other arithmetic, inner_pair(): delta_part = jnp.sum(shadow * residual)  9.11 us
  transfers between devices with their start and end apart: 12, of which 4 were waited for; matrix products, arithmetic and copies ran while one was open for 0% of the time, Pallas kernels for 0%

commit v1 on v0

--- a/solution.py
+++ b/solution.py
@@ -60,7 +60,7 @@
 def inner_pair(residual, shadow):
     gamma_part = jnp.sum(residual * residual)
     delta_part = jnp.sum(shadow * residual)
-    return lax.psum((gamma_part, delta_part), ("gx", "gy"))
+    return lax.psum(lax.psum((gamma_part, delta_part), "gy"), "gx")
 
 
 def shards(source, density):

time: 293 us -> 250 us (0.85)
  blocking collectives: 214 us -> 172 us
    psum x2 -> x4, blocking collectives: 214 us -> 172 us  [inner_pair(): return lax.psum(lax.psum((gamma_part, delta_part), 'gy'), 'gx')]
  transfers between devices with their start and end apart: 12 -> 12, of which waited for: 4 -> 4; matrix products, arithmetic and copies ran while one was open for 0% -> 1% of each run, Pallas kernels for 0% -> 0%
where the time goes in v1:
time: 250 us; the launch traced here: 249 us
  blocking collectives  172 us (69%)
  starting transfers between devices  34.8 us (14%)
  other arithmetic  19.3 us (8%)
  waiting for transfers between devices  14.9 us (6%)
  between operations  6.36 us (3%)
    psum x4, blocking collectives, inner_pair(): return lax.psum(lax.psum((gamma_part, delta_part), 'gy'), 'gx')  172 us
    ppermute x6, starting transfers between devices, extended(): before = lax.ppermute(last, axis, up)  21.9 us
    ppermute x6, waiting for transfers between devices, extended(): after = lax.ppermute(initial, axis, down)  14.9 us
    ppermute x6, starting transfers between devices, extended(): after = lax.ppermute(initial, axis, down)  12.9 us
    reduce_sum x2, other arithmetic, inner_pair(): delta_part = jnp.sum(shadow * residual)  9 us
  transfers between devices with their start and end apart: 12, of which 4 were waited for; matrix products, arithmetic and copies ran while one was open for 1% of the time, Pallas kernels for 0%

profile of v1, /device:TPU:1, one launch (start us, length us, event | category | flops | bytes accessed | tf_op | source)
XLA Modules:
  0.0 249.3 jit_solution(16119182951761778702)
XLA Ops:
  1.6 4.9 %collective-permute-start.1 = (f32[1,128,256]{2,1,0:T(8,128)S(1)}, f32[1,128,256]{2,1,0:T(8,128)S(1)}, u32[]{:S(2)}, u32[]{:S(2)}) collective-permute-start(f32[1,128,256]{2,1,0:T(8,128)S(1)} %get-tuple-element.34), channel_id=1, source_target_pairs={{0,16},{16,32},{32,48},{48,64},{64,80},{80,96},{96,112},{112,128},... | collective-permute-start | bytes 393224 | tf_op jit(solution)/shard_map/ppermute | solution.py:16
  6.6 5.1 %collective-permute-start = (f32[1,128,256]{2,1,0:T(8,128)S(1)}, f32[1,128,256]{2,1,0:T(8,128)S(1)}, u32[]{:S(2)}, u32[]{:S(2)}) collective-permute-start(f32[1,128,256]{2,1,0:T(8,128)S(1)} %get-tuple-element.33), channel_id=1, source_target_pairs={{16,0},{32,16},{48,32},{64,48},{80,64},{96,80},{112,96},{128,112},... | collective-permute-start | bytes 393224 | tf_op jit(solution)/shard_map/ppermute | solution.py:17
  11.7 1.3 constant_dynamic-update-slice_fusion.1
  13.1 2.9 %collective-permute-start.3 = (f32[10,1,256]{2,1,0:T(1,128)S(1)}, f32[10,1,256]{2,1,0:T(1,128)S(1)}, u32[]{:S(2)}, u32[]{:S(2)}) collective-permute-start(f32[10,1,256]{2,1,0:T(1,128)S(1)} %get-tuple-element.27), channel_id=1, source_target_pairs={{0,1},{1,2},{2,3},{3,4},{4,5},{5,6},{6,7},{7,8},{8,9},{9,10},{10,1... | collective-permute-start | bytes 30728 | tf_op jit(solution)/shard_map/ppermute | solution.py:16
  16.0 1.3 collective-permute-start.2
  17.3 3.1 %collective-permute-done.2 = f32[10,1,256]{2,1,0:T(1,128)S(1)} collective-permute-done((f32[10,1,256]{2,1,0:T(1,128)S(1)}, f32[10,1,256]{2,1,0:T(1,128)S(1)}, u32[]{:S(2)}, u32[]{:S(2)}) %collective-permute-start.2) | collective-permute-done | bytes 10272 | tf_op jit(solution)/shard_map/ppermute | solution.py:17
  21.2 2.2 fusion.43
  23.5 3.3 %collective-permute-start.5 = (f32[1,128,256]{2,1,0:T(8,128)S(1)}, f32[1,128,256]{2,1,0:T(8,128)S(1)}, u32[]{:S(2)}, u32[]{:S(2)}) collective-permute-start(f32[1,128,256]{2,1,0:T(8,128)S(1)} %get-tuple-element.31), channel_id=1, source_target_pairs={{0,16},{16,32},{32,48},{48,64},{64,80},{80,96},{96,112},{112,128},... | collective-permute-start | bytes 393224 | tf_op jit(solution)/shard_map/ppermute | solution.py:16
  26.8 1.9 collective-permute-start.4
  28.8 4.3 %collective-permute-done.4 = f32[1,128,256]{2,1,0:T(8,128)S(1)} collective-permute-done((f32[1,128,256]{2,1,0:T(8,128)S(1)}, f32[1,128,256]{2,1,0:T(8,128)S(1)}, u32[]{:S(2)}, u32[]{:S(2)}) %collective-permute-start.4) | collective-permute-done | bytes 131104 | tf_op jit(solution)/shard_map/ppermute | solution.py:17
  33.1 3.1 %collective-permute-start.7 = (f32[10,1,256]{2,1,0:T(1,128)S(1)}, f32[10,1,256]{2,1,0:T(1,128)S(1)}, u32[]{:S(2)}, u32[]{:S(2)}) collective-permute-start(f32[10,1,256]{2,1,0:T(1,128)S(1)} %get-tuple-element.25), channel_id=1, source_target_pairs={{0,1},{1,2},{2,3},{3,4},{4,5},{5,6},{6,7},{7,8},{8,9},{9,10},{10,1... | collective-permute-start | bytes 30728 | tf_op jit(solution)/shard_map/ppermute | solution.py:16
  37.6 3.1 %collective-permute-done.6 = f32[10,1,256]{2,1,0:T(1,128)S(1)} collective-permute-done((f32[10,1,256]{2,1,0:T(1,128)S(1)}, f32[10,1,256]{2,1,0:T(1,128)S(1)}, u32[]{:S(2)}, u32[]{:S(2)}) %collective-permute-start.6) | collective-permute-done | bytes 10272 | tf_op jit(solution)/shard_map/ppermute | solution.py:17
  41.4 3.3 %multiply_reduce_fusion.2 = (f32[]{:T(128)}, f32[]{:T(128)}, f32[8,128,256]{2,1,0:T(8,128)S(1)}) fusion(f32[8,128,256]{2,1,0:T(8,128)S(1)} %get-tuple-element.17, f32[8,128,256]{2,1,0:T(8,128)S(1)} %get-tuple-element.18, f32[10,130,258]{2,1,0:T(8,128)S(1)} %select_maximum_fusion.4, f32[8,128,256]{2,1,0:T(8,128)S(1)} %copy-done, ...), kind=kLoop, calls=%fused_computation.84 | loop fusion | flops 10485758 | bytes 12079112 | tf_op jit(solution)/shard_map/reduce_sum | solution.py:62
  45.0 3.2 %collective-permute-start.9 = (f32[1,128,256]{2,1,0:T(8,128)S(1)}, f32[1,128,256]{2,1,0:T(8,128)S(1)}, u32[]{:S(2)}, u32[]{:S(2)}) collective-permute-start(f32[1,128,256]{2,1,0:T(8,128)S(1)} %get-tuple-element.29), channel_id=1, source_target_pairs={{0,16},{16,32},{32,48},{48,64},{64,80},{80,96},{96,112},{112,128},... | collective-permute-start | bytes 393224 | tf_op jit(solution)/shard_map/ppermute | solution.py:16
  48.2 1.9 collective-permute-start.8
  50.1 4.3 %collective-permute-done.8 = f32[1,128,256]{2,1,0:T(8,128)S(1)} collective-permute-done((f32[1,128,256]{2,1,0:T(8,128)S(1)}, f32[1,128,256]{2,1,0:T(8,128)S(1)}, u32[]{:S(2)}, u32[]{:S(2)}) %collective-permute-start.8) | collective-permute-done | bytes 131104 | tf_op jit(solution)/shard_map/ppermute | solution.py:17
  55.1 4.4 %collective-permute-start.11 = (f32[10,1,256]{2,1,0:T(1,128)}, f32[10,1,256]{2,1,0:T(1,128)S(1)}, u32[]{:S(2)}, u32[]{:S(2)}) collective-permute-start(f32[10,1,256]{2,1,0:T(1,128)} %get-tuple-element.23), channel_id=1, source_target_pairs={{0,1},{1,2},{2,3},{3,4},{4,5},{5,6},{6,7},{7,8},{8,9},{9,10},{10,1... | collective-permute-start | bytes 30728 | tf_op jit(solution)/shard_map/ppermute | solution.py:16
  60.9 31.4 %all-reduce.6 = (f32[]{:T(128)}, f32[]{:T(128)}) all-reduce(f32[]{:T(128)} %get-tuple-element.5, f32[]{:T(128)} %get-tuple-element.4), channel_id=1, replica_groups=mesh['gx'=32,'gy'=16] {'gy'}, use_global_device_ids=true, to_apply=%region_1.2 | all-reduce | flops 2 | bytes 16 | tf_op jit(solution)/shard_map/psum | solution.py:63
  92.3 58.1 %all-reduce.4 = (f32[]{:T(128)}, f32[]{:T(128)}) all-reduce(f32[]{:T(128)} %get-tuple-element.12, f32[]{:T(128)} %get-tuple-element.13), channel_id=1, replica_groups=mesh['gx'=32,'gy'=16] {'gx'}, use_global_device_ids=true, to_apply=%region_2.3 | all-reduce | flops 2 | bytes 16 | tf_op jit(solution)/shard_map/psum | solution.py:63
  151.6 2.2 select_maximum_fusion
  153.8 5.7 %multiply_reduce_fusion = (f32[]{:T(128)}, f32[]{:T(128)}, f32[8,128,256]{2,1,0:T(8,128)}) fusion(f32[8,128,256]{2,1,0:T(8,128)S(1)} %copy-done.5, f32[8,128,256]{2,1,0:T(8,128)} %copy-done.6, f32[]{:T(128)S(6)} %div.36, f32[8,128,256]{2,1,0:T(8,128)S(1)} %get-tuple-element.18, f32[10,130,258]{2,1,0:T(8,128)S(1)} %select_maximum_fusion, ...), kind=kLoop, calls=%fused_computation.81 | loop fusion | flops 11534334 | bytes 13127692 | tf_op jit(solution)/shard_map/reduce_sum | solution.py:62
  159.5 29.2 %all-reduce.5 = (f32[]{:T(128)}, f32[]{:T(128)}) all-reduce(f32[]{:T(128)} %get-tuple-element.3, f32[]{:T(128)} %get-tuple-element.2), channel_id=1, replica_groups=mesh['gx'=32,'gy'=16] {'gy'}, use_global_device_ids=true, to_apply=%region_7.8 | all-reduce | flops 2 | bytes 16 | tf_op jit(solution)/shard_map/psum | solution.py:63
  188.7 52.8 %all-reduce.3 = (f32[]{:T(128)}, f32[]{:T(128)}) all-reduce(f32[]{:T(128)} %get-tuple-element.10, f32[]{:T(128)} %get-tuple-element.11), channel_id=1, replica_groups=mesh['gx'=32,'gy'=16] {'gx'}, use_global_device_ids=true, to_apply=%region_8.9 | all-reduce | flops 2 | bytes 16 | tf_op jit(solution)/shard_map/psum | solution.py:63
  245.7 3.6 %multiply_subtract_fusion = (f32[8,128,256]{2,1,0:T(8,128)}, f32[8,128,256]{2,1,0:T(8,128)}) fusion(f32[8,128,256]{2,1,0:T(8,128)} %get-tuple-element.14, f32[8,128,256]{2,1,0:T(8,128)} %copy-done.6, f32[]{:T(128)S(6)} %div.37, f32[]{:T(128)S(6)} %div.39, f32[8,128,256]{2,1,0:T(8,128)} %copy-done.4, f32[]{:T(128)S(6)} %div.36, ...), kind=kLoop, calls=%fused_computation.79 | loop fusion | flops 3145728 | bytes 6291468 | tf_op jit(solution)/shard_map/sub | solution.py:90
  (45 shorter events, 6.0 us)
Async XLA Ops:
  1.6 10.1 %collective-permute-start.1 = (f32[1,128,256]{2,1,0:T(8,128)S(1)}, f32[1,128,256]{2,1,0:T(8,128)S(1)}, u32[]{:S(2)}, u32[]{:S(2)}) collective-permute-start(f32[1,128,256]{2,1,0:T(8,128)S(1)} %get-tuple-element.34), channel_id=1, source_target_pairs={{0,16},{16,32},{32,48},{48,64},{64,80},{80,96},{96,112},{112,128},... | collective-permute-start | bytes 393224 | tf_op jit(solution)/shard_map/ppermute | solution.py:16
  6.6 6.5 %collective-permute-start = (f32[1,128,256]{2,1,0:T(8,128)S(1)}, f32[1,128,256]{2,1,0:T(8,128)S(1)}, u32[]{:S(2)}, u32[]{:S(2)}) collective-permute-start(f32[1,128,256]{2,1,0:T(8,128)S(1)} %get-tuple-element.33), channel_id=1, source_target_pairs={{16,0},{32,16},{48,32},{64,48},{80,64},{96,80},{112,96},{128,112},... | collective-permute-start | bytes 393224 | tf_op jit(solution)/shard_map/ppermute | solution.py:17
  13.1 8.1 %copy-start = (f32[8,128,256]{2,1,0:T(8,128)S(1)}, f32[8,128,256]{2,1,0:T(8,128)}, u32[]{:S(2)}) copy-start(f32[8,128,256]{2,1,0:T(8,128)} %param.3) | copy-start | bytes 3145732
  13.1 8.1 %copy-start.11 = (f32[8,128,256]{2,1,0:T(8,128)S(1)}, f32[8,128,256]{2,1,0:T(8,128)}, u32[]{:S(2)}) copy-start(f32[8,128,256]{2,1,0:T(8,128)} %param.2) | copy-start | bytes 3145732
  13.1 4.2 %collective-permute-start.3 = (f32[10,1,256]{2,1,0:T(1,128)S(1)}, f32[10,1,256]{2,1,0:T(1,128)S(1)}, u32[]{:S(2)}, u32[]{:S(2)}) collective-permute-start(f32[10,1,256]{2,1,0:T(1,128)S(1)} %get-tuple-element.27), channel_id=1, source_target_pairs={{0,1},{1,2},{2,3},{3,4},{4,5},{5,6},{6,7},{7,8},{8,9},{9,10},{10,1... | collective-permute-start | bytes 30728 | tf_op jit(solution)/shard_map/ppermute | solution.py:16
  16.0 4.4 %collective-permute-start.2 = (f32[10,1,256]{2,1,0:T(1,128)S(1)}, f32[10,1,256]{2,1,0:T(1,128)S(1)}, u32[]{:S(2)}, u32[]{:S(2)}) collective-permute-start(f32[10,1,256]{2,1,0:T(1,128)S(1)} %get-tuple-element.28), channel_id=1, source_target_pairs={{1,0},{2,1},{3,2},{4,3},{5,4},{6,5},{7,6},{8,7},{9,8},{10,9},{11,1... | collective-permute-start | bytes 30728 | tf_op jit(solution)/shard_map/ppermute | solution.py:17
  23.4 18.0 %copy-start.4 = (f32[8,128,256]{2,1,0:T(8,128)}, f32[8,128,256]{2,1,0:T(8,128)S(1)}, u32[]{:S(2)}) copy-start(f32[8,128,256]{2,1,0:T(8,128)S(1)} %get-tuple-element.17) | copy-start | bytes 3145732
  23.4 18.0 %copy-start.7 = (f32[8,128,256]{2,1,0:T(8,128)}, f32[8,128,256]{2,1,0:T(8,128)S(1)}, u32[]{:S(2)}) copy-start(f32[8,128,256]{2,1,0:T(8,128)S(1)} %get-tuple-element.19) | copy-start | bytes 3145732
  23.4 18.0 %copy-start.8 = (f32[8,128,256]{2,1,0:T(8,128)}, f32[8,128,256]{2,1,0:T(8,128)S(1)}, u32[]{:S(2)}) copy-start(f32[8,128,256]{2,1,0:T(8,128)S(1)} %get-tuple-element.20) | copy-start | bytes 3145732
  23.5 5.3 %collective-permute-start.5 = (f32[1,128,256]{2,1,0:T(8,128)S(1)}, f32[1,128,256]{2,1,0:T(8,128)S(1)}, u32[]{:S(2)}, u32[]{:S(2)}) collective-permute-start(f32[1,128,256]{2,1,0:T(8,128)S(1)} %get-tuple-element.31), channel_id=1, source_target_pairs={{0,16},{16,32},{32,48},{48,64},{64,80},{80,96},{96,112},{112,128},... | collective-permute-start | bytes 393224 | tf_op jit(solution)/shard_map/ppermute | solution.py:16
  26.8 6.3 %collective-permute-start.4 = (f32[1,128,256]{2,1,0:T(8,128)S(1)}, f32[1,128,256]{2,1,0:T(8,128)S(1)}, u32[]{:S(2)}, u32[]{:S(2)}) collective-permute-start(f32[1,128,256]{2,1,0:T(8,128)S(1)} %get-tuple-element.32), channel_id=1, source_target_pairs={{16,0},{32,16},{48,32},{64,48},{80,64},{96,80},{112,96},{128,112},... | collective-permute-start | bytes 393224 | tf_op jit(solution)/shard_map/ppermute | solution.py:17
  33.1 4.4 %collective-permute-start.7 = (f32[10,1,256]{2,1,0:T(1,128)S(1)}, f32[10,1,256]{2,1,0:T(1,128)S(1)}, u32[]{:S(2)}, u32[]{:S(2)}) collective-permute-start(f32[10,1,256]{2,1,0:T(1,128)S(1)} %get-tuple-element.25), channel_id=1, source_target_pairs={{0,1},{1,2},{2,3},{3,4},{4,5},{5,6},{6,7},{7,8},{8,9},{9,10},{10,1... | collective-permute-start | bytes 30728 | tf_op jit(solution)/shard_map/ppermute | solution.py:16
  36.3 4.4 %collective-permute-start.6 = (f32[10,1,256]{2,1,0:T(1,128)S(1)}, f32[10,1,256]{2,1,0:T(1,128)S(1)}, u32[]{:S(2)}, u32[]{:S(2)}) collective-permute-start(f32[10,1,256]{2,1,0:T(1,128)S(1)} %get-tuple-element.26), channel_id=1, source_target_pairs={{1,0},{2,1},{3,2},{4,3},{5,4},{6,5},{7,6},{8,7},{9,8},{10,9},{11,1... | collective-permute-start | bytes 30728 | tf_op jit(solution)/shard_map/ppermute | solution.py:17
  44.8 10.4 %copy-start.6 = (f32[8,128,256]{2,1,0:T(8,128)}, f32[8,128,256]{2,1,0:T(8,128)S(1)}, u32[]{:S(2)}) copy-start(f32[8,128,256]{2,1,0:T(8,128)S(1)} %get-tuple-element.15) | copy-start | bytes 3145732
  44.9 9.5 %copy-start.2 = (f32[8,128,256]{2,1,0:T(8,128)}, f32[8,128,256]{2,1,0:T(8,128)S(1)}, u32[]{:S(2)}) copy-start(f32[8,128,256]{2,1,0:T(8,128)S(1)} %mul.118) | copy-start | bytes 3145732
  45.0 5.2 %collective-permute-start.9 = (f32[1,128,256]{2,1,0:T(8,128)S(1)}, f32[1,128,256]{2,1,0:T(8,128)S(1)}, u32[]{:S(2)}, u32[]{:S(2)}) collective-permute-start(f32[1,128,256]{2,1,0:T(8,128)S(1)} %get-tuple-element.29), channel_id=1, source_target_pairs={{0,16},{16,32},{32,48},{48,64},{64,80},{80,96},{96,112},{112,128},... | collective-permute-start | bytes 393224 | tf_op jit(solution)/shard_map/ppermute | solution.py:16
  48.2 6.3 %collective-permute-start.8 = (f32[1,128,256]{2,1,0:T(8,128)S(1)}, f32[1,128,256]{2,1,0:T(8,128)S(1)}, u32[]{:S(2)}, u32[]{:S(2)}) collective-permute-start(f32[1,128,256]{2,1,0:T(8,128)S(1)} %get-tuple-element.30), channel_id=1, source_target_pairs={{16,0},{32,16},{48,32},{64,48},{80,64},{96,80},{112,96},{128,112},... | collective-permute-start | bytes 393224 | tf_op jit(solution)/shard_map/ppermute | solution.py:17
  54.5 0.7 copy-start.9
  55.1 96.4 %collective-permute-start.11 = (f32[10,1,256]{2,1,0:T(1,128)}, f32[10,1,256]{2,1,0:T(1,128)S(1)}, u32[]{:S(2)}, u32[]{:S(2)}) collective-permute-start(f32[10,1,256]{2,1,0:T(1,128)} %get-tuple-element.23), channel_id=1, source_target_pairs={{0,1},{1,2},{2,3},{3,4},{4,5},{5,6},{6,7},{7,8},{8,9},{9,10},{10,1... | collective-permute-start | bytes 30728 | tf_op jit(solution)/shard_map/ppermute | solution.py:16
  59.6 92.0 %collective-permute-start.10 = (f32[10,1,256]{2,1,0:T(1,128)}, f32[10,1,256]{2,1,0:T(1,128)S(1)}, u32[]{:S(2)}, u32[]{:S(2)}) collective-permute-start(f32[10,1,256]{2,1,0:T(1,128)} %get-tuple-element.24), channel_id=1, source_target_pairs={{1,0},{2,1},{3,2},{4,3},{5,4},{6,5},{7,6},{8,7},{9,8},{10,9},{11,1... | collective-permute-start | bytes 30728 | tf_op jit(solution)/shard_map/ppermute | solution.py:17
  151.5 2.2 copy-start.1
  151.6 2.2 copy-start.3
  151.6 2.2 copy-start.5
  151.6 2.2 copy-start.10
